TPU v7x, 512 devices: a whole 4x4x16 slice. The times are simulated.
512 devices in a mesh: seq: 64 (over y, z), head: 8 (over x, core).
Axes of the slice: x: 4, y: 4, z: 16, core: 2. Of those that a mesh axis runs over, the one named last changes fastest.
Arguments:
- queries: bfloat16 [65536, 2048], P(('seq', 'head')), may hold values from -135 to 135
- keys: bfloat16 [65536, 2048], P(('seq', 'head')), may hold values from -4.5 to 4.5
- values: bfloat16 [65536, 2048], P(('seq', 'head')), may hold values from -4.5 to 4.5
- doc_ids: int32 [65536], P(('seq', 'head')), may hold values from 0 to 127, never falling along the last dimension, each value on 1 to 1025 neighbouring positions
Outputs:
- attended: bfloat16 [65536, 2048], P(('seq', 'head'))
Inputs may be any that keep to these rules, and one draw needn't show every extreme that they name: `doc_ids`: never falling; every id from 0 to 127 names 1 to 1025 tokens, and one names exactly 1025.
All inputs are finite; a program needn't handle non-finite values.
Results may differ from a plain program's by a relative error of at most 0.0045.
Values may be sent and summed in bfloat16 or wider, within the bound.
No kernel may reach another device: no remote copies, remote signals or barrier semaphores. Data moves between devices by JAX's collectives and lax.ppermute only.
A program may use at most 64 MiB of HBM per device.

v0:
```python
import math

import jax
import jax.numpy as jnp
from jax import lax
from jax.sharding import PartitionSpec as P

HD = 128
SPAN = 1


def passed_along(value, axis, steps):
    count = lax.axis_size(axis)
    initial, last = (max(0, -steps), min(count, count - steps))
    return lax.ppermute(value, axis, [(source, source + steps) for source in range(initial, last)])


def score_tiles(query_rows, key_rows, value_rows, query_ids, key_ids):
    row_count = query_rows.shape[0]
    head_count = query_rows.shape[1] // HD
    same_doc = query_ids[:, None] == key_ids[None, :]
    score_scale = 1.0 / math.sqrt(HD)

    def live_tile():
        outputs, maxima, sums = ([], [], [])
        for head_index in range(head_count):
            lower_col = head_index * HD
            upper_col = lower_col + HD
            raw_scores = lax.dot_general(
                query_rows[:, lower_col:upper_col],
                key_rows[:, lower_col:upper_col],
                (((1,), (1,)), ((), ())),
                preferred_element_type=jnp.float32,
            )
            raw_max = jnp.max(jnp.where(same_doc, raw_scores, -1e30), axis=1)
            weights = jnp.exp(
                jnp.where(same_doc, (raw_scores - raw_max[:, None]) * score_scale, -1e30)
            )
            sums.append(jnp.sum(weights, axis=1))
            maxima.append(jnp.where(raw_max > -1e29, raw_max * score_scale, -1e30))
            outputs.append(
                jnp.dot(
                    weights.astype(jnp.bfloat16),
                    value_rows[:, lower_col:upper_col],
                    preferred_element_type=jnp.float32,
                )
            )
        return (jnp.concatenate(outputs, axis=1), jnp.stack(maxima), jnp.stack(sums))

    def dead_tile():
        return (
            jnp.zeros((row_count, head_count * HD), jnp.float32),
            jnp.full((head_count, row_count), -1e30, jnp.float32),
            jnp.zeros((head_count, row_count), jnp.float32),
        )

    return lax.cond(jnp.any(same_doc), live_tile, dead_tile)


def merge_partials(partials):
    overall = partials[0][1]
    for entry in partials[1:]:
        overall = jnp.maximum(overall, entry[1])
    row_count = partials[0][0].shape[0]
    head_count = overall.shape[0]
    numerator = jnp.zeros((row_count, head_count, HD), jnp.float32)
    denominator = jnp.zeros((head_count, row_count), jnp.float32)
    for partial_value, tile_max, totals in partials:
        factor = jnp.exp(tile_max - overall)
        denominator = denominator + factor * totals
        numerator = (
            numerator
            + partial_value.reshape(row_count, head_count, HD) * jnp.transpose(factor)[:, :, None]
        )
    result = numerator / jnp.transpose(denominator)[:, :, None]
    return result.reshape(row_count, head_count * HD).astype(jnp.bfloat16)


def fetch_upper(payload):
    return [passed_along(payload, "seq", -(0 + 1))]


def near_table(own_ids, position, block_count):
    table = {0: own_ids}
    for offset in list(range(-SPAN, 0)) + list(range(1, SPAN + 1)):
        moved = passed_along(own_ids, "seq", -offset)
        neighbour = position + offset
        inside = (neighbour >= 0) & (neighbour < block_count)
        table[offset] = jnp.where(inside, moved, -1)
    return table


def per_device(queries, keys, values, doc_ids):
    own_ids = lax.all_gather(doc_ids, "head", axis=0, tiled=True)
    query_rows, key_rows, value_rows = (
        lax.all_to_all(queries, "head", split_axis=1, concat_axis=0, tiled=True),
        lax.all_to_all(keys, "head", split_axis=1, concat_axis=0, tiled=True),
        lax.all_to_all(values, "head", split_axis=1, concat_axis=0, tiled=True),
    )
    position = lax.axis_index("seq")
    block_count = lax.axis_size("seq")
    id_table = near_table(own_ids, position, block_count)
    partials = [score_tiles(query_rows, key_rows, value_rows, own_ids, own_ids)]
    upper_blocks = fetch_upper(jnp.stack([query_rows, key_rows, value_rows]))
    above = upper_blocks[0]
    far_ids = id_table[1]
    partials.append(score_tiles(query_rows, above[1], above[2], own_ids, far_ids))
    back_out, back_max, back_total = score_tiles(above[0], key_rows, value_rows, far_ids, own_ids)
    got_out, got_max, got_total = passed_along((back_out, back_max, back_total), "seq", 1)
    got_max = jnp.where(position >= 1, got_max, -1e30)
    partials.append((got_out, got_max, got_total))
    attended_rows = merge_partials(partials)
    return lax.all_to_all(attended_rows, "head", split_axis=0, concat_axis=1, tiled=True)


def solution(mesh):
    return jax.shard_map(
        per_device,
        mesh=mesh,
        in_specs=(
            P(("seq", "head"), None),
            P(("seq", "head"), None),
            P(("seq", "head"), None),
            P(("seq", "head")),
        ),
        out_specs=P(("seq", "head"), None),
        check_vma=False,
    )
```

profile of v0, /device:TPU:24, one launch (start us, length us, event | category | flops | bytes accessed | tf_op | source)
XLA Modules:
  0.0 149.4 jit_solution(15851195810695396607)
XLA Ops:
  0.0 1.9 %copy.27 = bf16[16,8,8,256]{3,2,0,1:T(8,128)(2,1)} copy(bf16[16,8,8,256]{3,2,1,0:T(8,128)(2,1)} %bitcast.91) | data formatting | bytes 1048576 | tf_op jit(solution)/shard_map/all_to_all | solution.py:96
  1.9 4.4 %all-to-all-start = ((bf16[128,8,256]{2,0,1:T(8,128)(2,1)}), bf16[128,8,256]{2,0,1:T(8,128)(2,1)S(1)}, u32[]{:S(2)}, u32[]{:S(2)}) async-start(bf16[128,8,256]{2,0,1:T(8,128)(2,1)} %bitcast.78), calls=%async_computation | async-start | bytes 1048576 | tf_op jit(solution)/shard_map/all_to_all | solution.py:96
  6.4 1.9 %copy.26 = bf16[16,8,8,256]{3,2,0,1:T(8,128)(2,1)} copy(bf16[16,8,8,256]{3,2,1,0:T(8,128)(2,1)} %bitcast.92) | data formatting | bytes 1048576 | tf_op jit(solution)/shard_map/all_to_all | solution.py:97
  8.2 8.5 %all-to-all-done = bf16[128,8,256]{2,0,1:T(8,128)(2,1)S(1)} async-done(((bf16[128,8,256]{2,0,1:T(8,128)(2,1)}), bf16[128,8,256]{2,0,1:T(8,128)(2,1)S(1)}, u32[]{:S(2)}, u32[]{:S(2)}) %all-to-all-start) | async-done | bytes 524320 | tf_op jit(solution)/shard_map/all_to_all | solution.py:96
  16.7 3.5 %all-to-all-start.1 = ((bf16[128,8,256]{2,0,1:T(8,128)(2,1)}), bf16[128,8,256]{2,0,1:T(8,128)(2,1)S(1)}, u32[]{:S(2)}, u32[]{:S(2)}) async-start(bf16[128,8,256]{2,0,1:T(8,128)(2,1)} %bitcast.77), calls=%async_computation.1 | async-start | bytes 1048576 | tf_op jit(solution)/shard_map/all_to_all | solution.py:97
  20.3 10.2 %all-to-all-done.1 = bf16[128,8,256]{2,0,1:T(8,128)(2,1)S(1)} async-done(((bf16[128,8,256]{2,0,1:T(8,128)(2,1)}), bf16[128,8,256]{2,0,1:T(8,128)(2,1)S(1)}, u32[]{:S(2)}, u32[]{:S(2)}) %all-to-all-start.1) | async-done | bytes 524320 | tf_op jit(solution)/shard_map/all_to_all | solution.py:97
  30.5 12.8 %all_to_all.76 = bf16[128,8,256]{2,0,1:T(8,128)(2,1)S(1)} all-to-all(bf16[128,8,256]{2,0,1:T(8,128)(2,1)S(1)} %bitcast.85), channel_id=1, replica_groups=mesh['seq'=64,'head'=8] {'head'}, dimensions={1} | all-to-all | bytes 1048576 | tf_op jit(solution)/shard_map/all_to_all | solution.py:98
  45.4 11.6 %collective-permute-start.1 = (bf16[3,1024,256]{2,1,0:T(8,128)(2,1)}, bf16[3,1024,256]{2,1,0:T(8,128)(2,1)}, u32[]{:S(2)}, u32[]{:S(2)}) collective-permute-start(bf16[3,1024,256]{2,1,0:T(8,128)(2,1)} %pad_maximum_fusion.9), channel_id=1, source_target_pairs={{8,0},{16,8},{24,16},{32,24},{40,32},{48,40},{56,48},{64,56},{72,6... | collective-permute-start | bytes 4718600 | tf_op jit(solution)/shard_map/ppermute | solution.py:15
  57.0 8.9 %all-gather = s32[8,1,128]{2,1,0:T(1,128)S(1)} all-gather(s32[1,1,128]{2,1,0:T(1,128)S(1)} %bitcast.108), channel_id=1, replica_groups=mesh['seq'=64,'head'=8] {'head'}, dimensions={0}, use_global_device_ids=true | all-gather | bytes 4608 | tf_op jit(solution)/shard_map/all_gather | solution.py:94
  65.9 2.9 %collective-permute-start = (s32[1024]{0:T(1024)S(1)}, s32[1024]{0:T(1024)S(1)}, u32[]{:S(2)}, u32[]{:S(2)}) collective-permute-start(s32[1024]{0:T(1024)S(1)} %bitcast.94), channel_id=1, source_target_pairs={{8,0},{16,8},{24,16},{32,24},{40,32},{48,40},{56,48},{64,56},{72,6... | collective-permute-start | bytes 12296 | tf_op jit(solution)/shard_map/ppermute | solution.py:15
  68.8 21.8 %collective-permute-done = s32[1024]{0:T(1024)S(1)} collective-permute-done((s32[1024]{0:T(1024)S(1)}, s32[1024]{0:T(1024)S(1)}, u32[]{:S(2)}, u32[]{:S(2)}) %collective-permute-start) | collective-permute-done | bytes 4128 | tf_op jit(solution)/shard_map/ppermute | solution.py:15
  90.6 3.2 %fusion.67 = (pred[]{:T(512)}, pred[]{:T(512)}, pred[]{:T(512)}, pred[1024,1024]{0,1:T(32,128)(4,1)S(1)}, pred[1024,1024]{0,1:T(32,128)(4,1)S(1)}, /*index=5*/pred[1024,1024]{0,1:T(32,128)(4,1)S(1)}) fusion(s32[1024]{0:T(1024)S(1)} %broadcast_select_fusion.1, s32[1024]{0:T(1024)S(1)} %bitcast.95), kind=kLoop, calls=%fused_computation.109 | loop fusion | flops 6291453 | bytes 3153923 | tf_op jit(solution)/shard_map/reduce_or | solution.py:57
  94.3 10.1 %conditional.5 = (f32[1024,256]{0,1:T(8,128)}, f32[2,1024]{1,0:T(2,128)S(1)}, f32[2,1024]{1,0:T(2,128)S(1)}) conditional(s32[]{:T(128)} %convert_element_type.32, () %tuple.33, (bf16[3,1024,256]{2,1,0:T(8,128)(2,1)}, bf16[1024,256]{1,0:T(8,128)(2,1)}, pred[1024,1024]{0,1:T(32,128)(4,1)S(1)}, bf16[1024,256]{1,0:T(8,128)(2,1)}) %tuple.66), branch_computations={%region_15.16_spmd, %region_16.21_spmd} | conditional | flops 1094981632 | bytes 43597904 | solution.py:57
  98.8 2.0 %fusion.40 = (f32[1024]{0:T(1024)S(1)}, f32[1024]{0:T(1024)S(1)}) fusion(pred[1024,1024]{0,1:T(32,128)(4,1)S(1)} %get-tuple-element.41, f32[1024,1024]{0,1:T(8,128)S(1)} %get-tuple-element.86, f32[1024]{0:T(1024)S(1)} %get-tuple-element.73, f32[1024,1024]{0,1:T(8,128)S(1)} %fusion.48, f32[1024]{0:T(1024)S(1)} %get-tuple-element.74), kind=kLoop, calls=%fused_computation.60 | loop fusion | flops 8386560 | bytes 9453568 | tf_op jit(solution)/shard_map/cond/branch_1_fun/reduce_sum | solution.py:39
  104.5 1.9 %collective-permute-start.3 = (f32[1024,256]{0,1:T(8,128)}, f32[1024,256]{0,1:T(8,128)}, u32[]{:S(2)}, u32[]{:S(2)}) collective-permute-start(f32[1024,256]{0,1:T(8,128)} %get-tuple-element.59), channel_id=1, source_target_pairs={{0,8},{8,16},{16,24},{24,32},{32,40},{40,48},{48,56},{56,64},{64,7... | collective-permute-start | bytes 3145736 | tf_op jit(solution)/shard_map/ppermute | solution.py:15
  106.4 1.9 %collective-permute-start.2 = (f32[2,1024]{1,0:T(2,128)S(1)}, f32[2,1024]{1,0:T(2,128)S(1)}, u32[]{:S(2)}, u32[]{:S(2)}) collective-permute-start(f32[2,1024]{1,0:T(2,128)S(1)} %get-tuple-element.57), channel_id=1, source_target_pairs={{0,8},{8,16},{16,24},{24,32},{32,40},{40,48},{48,56},{56,64},{64,7... | collective-permute-start | bytes 24584 | tf_op jit(solution)/shard_map/ppermute | solution.py:15
  108.4 1.9 %collective-permute-start.4 = (f32[2,1024]{1,0:T(2,128)S(1)}, f32[2,1024]{1,0:T(2,128)S(1)}, u32[]{:S(2)}, u32[]{:S(2)}) collective-permute-start(f32[2,1024]{1,0:T(2,128)S(1)} %get-tuple-element.62), channel_id=1, source_target_pairs={{0,8},{8,16},{16,24},{24,32},{32,40},{40,48},{48,56},{56,64},{64,7... | collective-permute-start | bytes 24584 | tf_op jit(solution)/shard_map/ppermute | solution.py:15
  111.5 8.4 %conditional.3 = (f32[1024,256]{0,1:T(8,128)S(1)}, f32[2,1024]{1,0:T(2,128)S(1)}, f32[2,1024]{1,0:T(2,128)S(1)}) conditional(s32[]{:T(128)} %convert_element_type.30, () %tuple.29, (bf16[1024,256]{1,0:T(8,128)(2,1)}, bf16[1024,256]{1,0:T(8,128)(2,1)}, pred[1024,1024]{0,1:T(32,128)(4,1)S(1)}, bf16[1024,256]{1,0:T(8,128)(2,1)}) %tuple.67), branch_computations={%region_1.2_spmd, %region_2.7_spmd} | conditional | flops 1094981632 | bytes 44646508 | solution.py:57
  111.7 1.8 %fusion.9 = f32[1024,1024]{0,1:T(8,128)S(1)} fusion(bf16[1024,256]{1,0:T(8,128)(2,1)} %get-tuple-element.36, bf16[1024,256]{1,0:T(8,128)(2,1)} %get-tuple-element.35), kind=kOutput, calls=%fused_computation.12 | convolution fusion | flops 268435456 | bytes 4718592 | tf_op jit(solution)/shard_map/cond/branch_1_fun/dot_general | solution.py:29
  115.1 2.0 %fusion = (f32[1024]{0:T(1024)S(1)}, f32[1024]{0:T(1024)S(1)}) fusion(pred[1024,1024]{0,1:T(32,128)(4,1)S(1)} %get-tuple-element.34, f32[1024,1024]{0,1:T(8,128)S(1)} %get-tuple-element.78, f32[1024]{0:T(1024)S(1)} %get-tuple-element.65, f32[1024,1024]{0,1:T(8,128)S(1)} %fusion.9, f32[1024]{0:T(1024)S(1)} %get-tuple-element.66), kind=kLoop, calls=%fused_computation.4 | loop fusion | flops 8386560 | bytes 9453568 | tf_op jit(solution)/shard_map/cond/branch_1_fun/reduce_sum | solution.py:39
  119.9 9.4 %conditional.4 = (f32[1024,256]{0,1:T(8,128)S(1)}, f32[2,1024]{1,0:T(2,128)S(1)}, f32[2,1024]{1,0:T(2,128)S(1)}) conditional(s32[]{:T(128)} %convert_element_type.31, () %tuple.31, (bf16[1024,256]{1,0:T(8,128)(2,1)}, bf16[3,1024,256]{2,1,0:T(8,128)(2,1)}, pred[1024,1024]{0,1:T(32,128)(4,1)S(1)}) %tuple.63), branch_computations={%region_8.9_spmd, %region_9.14_spmd} | conditional | flops 1094981632 | bytes 42549300 | solution.py:57
  124.5 2.0 %fusion.20 = (f32[1024]{0:T(1024)S(1)}, f32[1024]{0:T(1024)S(1)}) fusion(pred[1024,1024]{0,1:T(32,128)(4,1)S(1)} %get-tuple-element.38, f32[1024,1024]{0,1:T(8,128)S(1)} %get-tuple-element.83, f32[1024]{0:T(1024)S(1)} %get-tuple-element.69, f32[1024,1024]{0,1:T(8,128)S(1)} %fusion.29, f32[1024]{0:T(1024)S(1)} %get-tuple-element.70), kind=kLoop, calls=%fused_computation.31 | loop fusion | flops 8386560 | bytes 9453568 | tf_op jit(solution)/shard_map/cond/branch_1_fun/reduce_sum | solution.py:39
  129.3 4.1 %collective-permute-done.2 = f32[2,1024]{1,0:T(2,128)S(1)} collective-permute-done((f32[2,1024]{1,0:T(2,128)S(1)}, f32[2,1024]{1,0:T(2,128)S(1)}, u32[]{:S(2)}, u32[]{:S(2)}) %collective-permute-start.2) | collective-permute-done | bytes 8224 | tf_op jit(solution)/shard_map/ppermute | solution.py:15
  135.3 12.8 %all_to_all.77 = bf16[8,128,256]{2,1,0:T(8,128)(2,1)S(1)} all-to-all(bf16[8,128,256]{2,1,0:T(8,128)(2,1)S(1)} %bitcast.86), channel_id=1, replica_groups=mesh['seq'=64,'head'=8] {'head'}, dimensions={0} | all-to-all | bytes 1048576 | tf_op jit(solution)/shard_map/all_to_all | solution.py:113
  (58 shorter events, 25.0 us)
Async XLA Ops:
  0.0 20.2 %copy-start.9 = (bf16[128,2048]{1,0:T(8,128)(2,1)S(1)}, bf16[128,2048]{1,0:T(8,128)(2,1)}, u32[]{:S(2)}) copy-start(bf16[128,2048]{1,0:T(8,128)(2,1)} %param.12) | copy-start | bytes 1572868
  1.9 55.0 %copy-start.10 = (s32[128]{0:T(128)S(1)}, s32[128]{0:T(128)}, u32[]{:S(2)}) copy-start(s32[128]{0:T(128)} %param.13) | copy-start | bytes 1540
  1.9 14.8 %all-to-all-start = ((bf16[128,8,256]{2,0,1:T(8,128)(2,1)}), bf16[128,8,256]{2,0,1:T(8,128)(2,1)S(1)}, u32[]{:S(2)}, u32[]{:S(2)}) async-start(bf16[128,8,256]{2,0,1:T(8,128)(2,1)} %bitcast.78), calls=%async_computation | async-start | bytes 1048576 | tf_op jit(solution)/shard_map/all_to_all | solution.py:96
  16.7 73.9 %copy-start = (bf16[128,8,256]{2,0,1:T(8,128)(2,1)}, bf16[128,8,256]{2,0,1:T(8,128)(2,1)S(1)}, u32[]{:S(2)}) copy-start(bf16[128,8,256]{2,0,1:T(8,128)(2,1)S(1)} %all-to-all-done) | copy-start | bytes 1572868
  16.7 13.8 %all-to-all-start.1 = ((bf16[128,8,256]{2,0,1:T(8,128)(2,1)}), bf16[128,8,256]{2,0,1:T(8,128)(2,1)S(1)}, u32[]{:S(2)}, u32[]{:S(2)}) async-start(bf16[128,8,256]{2,0,1:T(8,128)(2,1)} %bitcast.77), calls=%async_computation.1 | async-start | bytes 1048576 | tf_op jit(solution)/shard_map/all_to_all | solution.py:97
  30.5 60.1 %copy-start.3 = (bf16[128,8,256]{2,0,1:T(8,128)(2,1)}, bf16[128,8,256]{2,0,1:T(8,128)(2,1)S(1)}, u32[]{:S(2)}) copy-start(bf16[128,8,256]{2,0,1:T(8,128)(2,1)S(1)} %all-to-all-done.1) | copy-start | bytes 1572868
  43.3 0.8 copy-start.6
  45.4 48.9 %collective-permute-start.1 = (bf16[3,1024,256]{2,1,0:T(8,128)(2,1)}, bf16[3,1024,256]{2,1,0:T(8,128)(2,1)}, u32[]{:S(2)}, u32[]{:S(2)}) collective-permute-start(bf16[3,1024,256]{2,1,0:T(8,128)(2,1)} %pad_maximum_fusion.9), channel_id=1, source_target_pairs={{8,0},{16,8},{24,16},{32,24},{40,32},{48,40},{56,48},{64,56},{72,6... | collective-permute-start | bytes 4718600 | tf_op jit(solution)/shard_map/ppermute | solution.py:15
  65.9 24.7 %collective-permute-start = (s32[1024]{0:T(1024)S(1)}, s32[1024]{0:T(1024)S(1)}, u32[]{:S(2)}, u32[]{:S(2)}) collective-permute-start(s32[1024]{0:T(1024)S(1)} %bitcast.94), channel_id=1, source_target_pairs={{8,0},{16,8},{24,16},{32,24},{40,32},{48,40},{56,48},{64,56},{72,6... | collective-permute-start | bytes 12296 | tf_op jit(solution)/shard_map/ppermute | solution.py:15
  94.4 2.8 %copy-start.4 = (bf16[1024,256]{1,0:T(8,128)(2,1)S(1)}, bf16[1024,256]{1,0:T(8,128)(2,1)}, u32[]{:S(2)}) copy-start(bf16[1024,256]{1,0:T(8,128)(2,1)} %get-tuple-element.43) | copy-start | bytes 1572868 | tf_op jit(solution)/shard_map/cond
  98.8 2.0 %copy-start.7 = (bf16[1024,256]{1,0:T(8,128)(2,1)S(1)}, bf16[1024,256]{1,0:T(8,128)(2,1)}, u32[]{:S(2)}) copy-start(bf16[1024,256]{1,0:T(8,128)(2,1)} %get-tuple-element.44) | copy-start | bytes 1572868 | tf_op jit(solution)/shard_map/cond
  104.5 29.0 %collective-permute-start.3 = (f32[1024,256]{0,1:T(8,128)}, f32[1024,256]{0,1:T(8,128)}, u32[]{:S(2)}, u32[]{:S(2)}) collective-permute-start(f32[1024,256]{0,1:T(8,128)} %get-tuple-element.59), channel_id=1, source_target_pairs={{0,8},{8,16},{16,24},{24,32},{32,40},{40,48},{48,56},{56,64},{64,7... | collective-permute-start | bytes 3145736 | tf_op jit(solution)/shard_map/ppermute | solution.py:15
  106.4 27.0 %collective-permute-start.2 = (f32[2,1024]{1,0:T(2,128)S(1)}, f32[2,1024]{1,0:T(2,128)S(1)}, u32[]{:S(2)}, u32[]{:S(2)}) collective-permute-start(f32[2,1024]{1,0:T(2,128)S(1)} %get-tuple-element.57), channel_id=1, source_target_pairs={{0,8},{8,16},{16,24},{24,32},{32,40},{40,48},{48,56},{56,64},{64,7... | collective-permute-start | bytes 24584 | tf_op jit(solution)/shard_map/ppermute | solution.py:15
  108.4 25.1 %collective-permute-start.4 = (f32[2,1024]{1,0:T(2,128)S(1)}, f32[2,1024]{1,0:T(2,128)S(1)}, u32[]{:S(2)}, u32[]{:S(2)}) collective-permute-start(f32[2,1024]{1,0:T(2,128)S(1)} %get-tuple-element.62), channel_id=1, source_target_pairs={{0,8},{8,16},{16,24},{24,32},{32,40},{40,48},{48,56},{56,64},{64,7... | collective-permute-start | bytes 24584 | tf_op jit(solution)/shard_map/ppermute | solution.py:15
  111.7 1.8 %copy-start.1 = (bf16[1024,256]{1,0:T(8,128)(2,1)S(1)}, bf16[1024,256]{1,0:T(8,128)(2,1)}, u32[]{:S(2)}) copy-start(bf16[1024,256]{1,0:T(8,128)(2,1)} %get-tuple-element.35) | copy-start | bytes 1572868 | tf_op jit(solution)/shard_map/cond
  111.7 1.8 %copy-start.5 = (bf16[1024,256]{1,0:T(8,128)(2,1)S(1)}, bf16[1024,256]{1,0:T(8,128)(2,1)}, u32[]{:S(2)}) copy-start(bf16[1024,256]{1,0:T(8,128)(2,1)} %get-tuple-element.36) | copy-start | bytes 1572868 | tf_op jit(solution)/shard_map/cond
  115.1 2.0 %copy-start.8 = (bf16[1024,256]{1,0:T(8,128)(2,1)S(1)}, bf16[1024,256]{1,0:T(8,128)(2,1)}, u32[]{:S(2)}) copy-start(bf16[1024,256]{1,0:T(8,128)(2,1)} %get-tuple-element.37) | copy-start | bytes 1572868 | tf_op jit(solution)/shard_map/cond
  119.9 3.0 %copy-start.2 = (bf16[1024,256]{1,0:T(8,128)(2,1)S(1)}, bf16[1024,256]{1,0:T(8,128)(2,1)}, u32[]{:S(2)}) copy-start(bf16[1024,256]{1,0:T(8,128)(2,1)} %get-tuple-element.39) | copy-start | bytes 1572868 | tf_op jit(solution)/shard_map/cond
where the time goes:
time: 150 us; the launch traced here: 149 us
  waiting for transfers between devices  44.7 us (30%)
  blocking collectives  34.5 us (23%)
  starting transfers between devices  28.2 us (19%)
  matrix products  17.7 us (12%)
  other arithmetic  13.4 us (9%)
  local copies, waits for them, and re-layouts  8.61 us (6%)
  between operations  1.88 us (1%)
    ppermute x5, waiting for transfers between devices, passed_along(): lax.ppermute(value, axis, [(source, source + steps) for source in range(i...  26 us
    ppermute x5, starting transfers between devices, passed_along(): lax.ppermute(value, axis, [(source, source + steps) for source in range(i...  20.2 us
    all_to_all x1, blocking collectives, per_device(): lax.all_to_all(attended_rows, 'head', split_axis=0, concat_axis=1, tiled=...  12.8 us
    all_to_all x1, blocking collectives, per_device(): lax.all_to_all(values, 'head', split_axis=1, concat_axis=0, tiled=True)  12.8 us
    all_to_all x1, waiting for transfers between devices, per_device(): lax.all_to_all(keys, 'head', split_axis=1, concat_axis=0, tiled=True)  10.2 us
    dot_general x6, matrix products, live_tile(): lax.dot_general(query_rows[:, lower_col:upper_col], key_rows[:, lower_col...  9.9 us
    all_gather x1, blocking collectives, per_device(): own_ids = lax.all_gather(doc_ids, 'head', axis=0, tiled=True)  8.9 us
    all_to_all x1, waiting for transfers between devices, per_device(): lax.all_to_all(queries, 'head', split_axis=1, concat_axis=0, tiled=True)  8.48 us
  transfers between devices with their start and end apart: 7, of which 5 were waited for; matrix products, arithmetic and copies ran while one was open for 15% of the time, Pallas kernels for 0%

commit v1 on v0

v1 whole, which is shorter than its diff:
```python
import math

import jax
import jax.numpy as jnp
from jax import lax
from jax.experimental import pallas as pl
from jax.experimental.pallas import tpu as pltpu
from jax.sharding import PartitionSpec as P

HD = 128
ROWS = 128
PARTS = 8
HEADS = 2
WIDE = HEADS * HD
TAGS = 16
PIECE = 2 * ROWS + TAGS
BLOCK = PARTS * ROWS
TILE = 2 * ROWS
TILES = BLOCK // TILE
BIG = 1e30
EXP2_SCALE = math.log2(math.e) / math.sqrt(HD)
HBM = pl.BlockSpec(memory_space=pltpu.HBM)
ANY = pl.BlockSpec(memory_space=pl.ANY)
SMEM = pl.BlockSpec(memory_space=pltpu.SMEM)
VMEM = pl.BlockSpec(memory_space=pltpu.VMEM)
LIMIT = pltpu.CompilerParams(vmem_limit_bytes=32 * 1024 * 1024)
F32 = jnp.float32
BF16 = jnp.bfloat16


def estimate(work):
    return pl.CostEstimate(flops=work << 30, bytes_accessed=work << 21, transcendentals=0)


def run_copies(pairs, sems):
    copies = [pltpu.make_async_copy(s, t, sems.at[i]) for i, (s, t) in enumerate(pairs)]
    for copy in copies:
        copy.start()
    return copies


def head_cols(h):
    return slice(h * HD, (h + 1) * HD)


def part_cols(p):
    return slice(p * WIDE, (p + 1) * WIDE)


def pack_kv_kernel(ids, keys, values, kv, sems):
    pairs = []
    for p in range(PARTS):
        pairs += [
            (keys.at[:, part_cols(p)], kv.at[p, 0:ROWS]),
            (values.at[:, part_cols(p)], kv.at[p, ROWS : 2 * ROWS]),
        ]
    copies = run_copies(pairs, sems)
    row = jnp.broadcast_to(ids[...].astype(F32), (TAGS, ROWS))
    tags = jnp.concatenate([row] * HEADS, axis=1).astype(BF16)
    for p in range(PARTS):
        kv[p, 2 * ROWS : PIECE, :] = tags
    for copy in copies:
        copy.wait()


def pack_kv(ids, keys, values):
    return pl.pallas_call(
        pack_kv_kernel,
        out_shape=jax.ShapeDtypeStruct((PARTS, PIECE, WIDE), BF16),
        in_specs=[VMEM, HBM, HBM],
        out_specs=VMEM,
        scratch_shapes=[pltpu.SemaphoreType.DMA((2 * PARTS,))],
        compiler_params=pltpu.CompilerParams(vmem_limit_bytes=61 * 1024 * 1024),
        name="pack_kv",
    )(ids, keys, values)


def pack_q_kernel(queries, qs, sems):
    copies = run_copies(
        [(queries.at[:, part_cols(p)], qs.at[p]) for p in range(PARTS)], sems
    )
    for copy in copies:
        copy.wait()


def pack_q(queries):
    return pl.pallas_call(
        pack_q_kernel,
        out_shape=jax.ShapeDtypeStruct((PARTS, ROWS, WIDE), BF16),
        in_specs=[HBM],
        out_specs=VMEM,
        scratch_shapes=[pltpu.SemaphoreType.DMA((PARTS,))],
        compiler_params=pltpu.CompilerParams(vmem_limit_bytes=61 * 1024 * 1024),
        cost_estimate=estimate(8),
        name="pack_q",
    )(queries)


def unpack_kernel(parts, out, sems):
    copies = run_copies([(parts.at[p], out.at[:, part_cols(p)]) for p in range(PARTS)], sems)
    for copy in copies:
        copy.wait()


def unpack(parts):
    return pl.pallas_call(
        unpack_kernel,
        out_shape=jax.ShapeDtypeStruct((ROWS, PARTS * WIDE), BF16),
        in_specs=[VMEM],
        out_specs=HBM,
        scratch_shapes=[pltpu.SemaphoreType.DMA((PARTS,))],
        compiler_params=LIMIT,
        name="unpack",
    )(parts)


def id_row(ref, p):
    return ref[p, 2 * ROWS : PIECE, 0:ROWS].astype(F32)[0:1, :]


def down_rows(row):
    return jnp.transpose(jnp.broadcast_to(row, (ROWS, ROWS)))


def tile_ids(ref, tile):
    return jnp.concatenate([id_row(ref, 2 * tile), id_row(ref, 2 * tile + 1)], axis=1)


def tile_rows(ref, tile, part, h):
    rows = slice(part * ROWS, (part + 1) * ROWS)
    return jnp.concatenate([ref[2 * tile + i, rows, head_cols(h)] for i in range(2)], axis=0)


def query_rows(ref, tile, h):
    return jnp.concatenate([ref[2 * tile + i, :, head_cols(h)] for i in range(2)], axis=0)


def scores_of(q, k):
    return lax.dot_general(q, k, (((1,), (1,)), ((), ())), preferred_element_type=F32)


def weigh(weights, v):
    ones = jnp.ones((v.shape[0], HD), BF16)
    return jnp.dot(
        weights.astype(BF16), jnp.concatenate([v, ones], axis=1), preferred_element_type=F32
    )


def wide(value):
    return jnp.concatenate([value, value], axis=1)


def own_kernel(kv, qs, q_ids, out_sum, out_total, out_max, scores):
    for p in range(PARTS):
        q_ids[p * ROWS : (p + 1) * ROWS, :] = down_rows(id_row(kv, p))
    for t in range(TILES):
        rows = slice(t * TILE, (t + 1) * TILE)
        tops = [None] * HEADS
        for k in range(TILES):
            same = wide(q_ids[rows, :]) == tile_ids(kv, k)
            bias = jnp.where(same, 0.0, -BIG)
            for h in range(HEADS):
                part = scores_of(query_rows(qs, t, h), tile_rows(kv, k, 0, h)) + bias
                scores[h, :, k * TILE : (k + 1) * TILE] = part
                best = jnp.maximum(part[:, :HD], part[:, HD:])
                tops[h] = best if k == 0 else jnp.maximum(tops[h], best)
        for h in range(HEADS):
            top = jnp.broadcast_to(jnp.max(tops[h], axis=1, keepdims=True), (TILE, HD))
            both = None
            for k in range(TILES):
                part = scores[h, :, k * TILE : (k + 1) * TILE]
                weights = jnp.exp2((part - wide(top)) * EXP2_SCALE)
                added = weigh(weights, tile_rows(kv, k, 1, h))
                both = added if k == 0 else both + added
            out_sum[rows, head_cols(h)] = both[:, :HD]
            out_total[rows, head_cols(h)] = both[:, HD:]
            out_max[rows, head_cols(h)] = top


def own_block(kv, qs):
    state = jax.ShapeDtypeStruct((BLOCK, WIDE), F32)
    return pl.pallas_call(
        own_kernel,
        out_shape=[jax.ShapeDtypeStruct((BLOCK, ROWS), F32), state, state, state],
        in_specs=[VMEM] * 2,
        out_specs=[VMEM] * 4,
        scratch_shapes=[pltpu.VMEM((HEADS, TILE, BLOCK), F32)],
        compiler_params=LIMIT,
        cost_estimate=estimate(8),
        name="own_block",
    )(kv, qs)


def near_kernel(place, up, down, qs, q_ids, own_sum, own_total, own_max, out, sum_, total, top_):
    sum_[...] = jnp.zeros_like(sum_)
    total[...] = jnp.zeros_like(total)
    top_[...] = jnp.full_like(top_, -BIG)
    lows = [jnp.max(q_ids[t * TILE : t * TILE + 1, :]) for t in range(TILES)]
    highs = [jnp.max(q_ids[(t + 1) * TILE - 1 : (t + 1) * TILE, :]) for t in range(TILES)]
    ids = [[tile_ids(ref, k) for k in range(TILES)] for ref in (up, down)]
    lasts = [jnp.max(row) for row in ids[0]]
    firsts = [jnp.min(row) for row in ids[1]]
    for side, ref in enumerate((up, down)):
        for k in range(TILES):
            k_ids = ids[side][k]
            for t in range(TILES):
                rows = slice(t * TILE, (t + 1) * TILE)
                if side:
                    live = (firsts[k] <= highs[t]) & (place[0] < place[1] - 1)
                else:
                    live = (lasts[k] >= lows[t]) & (place[0] > 0)

                @pl.when(live)
                def _(ref=ref, k=k, t=t, rows=rows, k_ids=k_ids):
                    bias = jnp.where(wide(q_ids[rows, :]) == k_ids, 0.0, -BIG)
                    for h in range(HEADS):
                        cols = head_cols(h)
                        scores = scores_of(query_rows(qs, t, h), tile_rows(ref, k, 0, h)) + bias
                        old = top_[rows, cols]
                        new = jnp.maximum(old, jnp.max(scores, axis=1, keepdims=True))
                        factor = jnp.exp2((old - new) * EXP2_SCALE)
                        weights = jnp.exp2((scores - wide(new)) * EXP2_SCALE)
                        both = weigh(weights, tile_rows(ref, k, 1, h))
                        sum_[rows, cols] = sum_[rows, cols] * factor + both[:, :HD]
                        total[rows, cols] = total[rows, cols] * factor + both[:, HD:]
                        top_[rows, cols] = new

    for p in range(PARTS):
        rows = slice(p * ROWS, (p + 1) * ROWS)
        best = jnp.maximum(top_[rows, :], own_max[rows, :])
        far = jnp.exp2((top_[rows, :] - best) * EXP2_SCALE)
        near = jnp.exp2((own_max[rows, :] - best) * EXP2_SCALE)
        value = near * own_sum[rows, :] + far * sum_[rows, :]
        scale = near * own_total[rows, :] + far * total[rows, :]
        out[p] = (value / scale).astype(BF16)


def near_blocks(place, up, down, qs, state):
    return pl.pallas_call(
        near_kernel,
        out_shape=jax.ShapeDtypeStruct((PARTS, ROWS, WIDE), BF16),
        in_specs=[SMEM] + [VMEM] * 7,
        out_specs=VMEM,
        scratch_shapes=[pltpu.VMEM((BLOCK, WIDE), F32)] * 3,
        compiler_params=LIMIT,
        cost_estimate=estimate(3),
        name="near_blocks",
    )(place, up, down, qs, *state)


def across_heads(value):
    return lax.all_to_all(value, "head", 0, 0, tiled=True)


def across_blocks(value, step):
    size = lax.axis_size("seq")
    return lax.ppermute(value, "seq", [(i, (i + step) % size) for i in range(size)])


def per_device(queries, keys, values, doc_ids):
    count = jnp.int32(lax.axis_size("seq"))
    place = jnp.stack([lax.axis_index("seq"), count]).astype(jnp.int32)
    kv = across_heads(pack_kv(doc_ids.reshape(1, ROWS), keys, values))
    kv, queries = lax.optimization_barrier((kv, queries))
    up, down = across_blocks(kv, 1), across_blocks(kv, -1)
    qs = across_heads(pack_q(queries))
    state = own_block(kv, qs)
    out = near_blocks(place, up, down, qs, state)
    return unpack(across_heads(out))


def solution(mesh):
    return jax.shard_map(
        per_device,
        mesh=mesh,
        in_specs=(
            P(("seq", "head"), None),
            P(("seq", "head"), None),
            P(("seq", "head"), None),
            P(("seq", "head")),
        ),
        out_specs=P(("seq", "head"), None),
        check_vma=False,
    )
```

time: 150 us -> 95.9 us (0.64)
  the two profiles are of different devices: /device:TPU:24 before, /device:TPU:1 now
where the time goes in v1:
time: 95.9 us; the launch traced here: 95.4 us
  blocking collectives  41.3 us (43%)
  waiting for transfers between devices  25.4 us (26%)
  starting transfers between devices  15.1 us (16%)
  Pallas kernels  13.4 us (14%)
    all_to_all x2, blocking collectives, across_heads(): return lax.all_to_all(value, 'head', 0, 0, tiled=True)  41.3 us
    ppermute x2, waiting for transfers between devices, across_blocks(): lax.ppermute(value, 'seq', [(i, (i + step) % size) for i in range(size)])  25.4 us
    ppermute x2, starting transfers between devices, across_blocks(): lax.ppermute(value, 'seq', [(i, (i + step) % size) for i in range(size)])  10.9 us
    all_to_all x1, starting transfers between devices, across_heads(): return lax.all_to_all(value, 'head', 0, 0, tiled=True)  4.15 us
    pallas_call x1, Pallas kernels, near_blocks(): pl.pallas_call(near_kernel, out_shape=jax.ShapeDtypeStruct((PARTS, ROWS,...  3.94 us
    pallas_call x1, Pallas kernels, own_block(): pl.pallas_call(own_kernel, out_shape=[jax.ShapeDtypeStruct((BLOCK, ROWS),...  3.63 us
    pallas_call x1, Pallas kernels, pack_kv(): pl.pallas_call(pack_kv_kernel, out_shape=jax.ShapeDtypeStruct((PARTS, PIE...  3.03 us
    pallas_call x1, Pallas kernels, pack_q(): pl.pallas_call(pack_q_kernel, out_shape=jax.ShapeDtypeStruct((PARTS, ROWS...  1.93 us
  transfers between devices with their start and end apart: 3, of which 2 were waited for; matrix products, arithmetic and copies ran while one was open for 0% of the time, Pallas kernels for 4%

profile of v1, /device:TPU:1, one launch (start us, length us, event | category | flops | bytes accessed | tf_op | source)
XLA Modules:
  0.0 95.4 jit_solution(7228757543709312970)
XLA Ops:
  0.0 3.0 %pack_kv.1 = bf16[8,272,256]{2,1,0:T(8,128)(2,1)} custom-call(s32[1,128]{1,0:T(1,128)} %bitcast.2, bf16[128,2048]{1,0:T(8,128)(2,1)} %keys.1, bf16[128,2048]{1,0:T(8,128)(2,1)} %values.1), custom_call_target="tpu_custom_call" | custom-call | tf_op jit(solution)/shard_map/pack_kv/pallas_call | solution.py:67
  3.0 26.4 %all_to_all.15.kv = bf16[8,272,256]{2,1,0:T(8,128)(2,1)S(1)} all-to-all(bf16[8,272,256]{2,1,0:T(8,128)(2,1)} %pack_kv.1), channel_id=1, replica_groups=mesh['seq'=64,'head'=8] {'head'}, dimensions={0} | all-to-all | bytes 2228224 | tf_op jit(solution)/shard_map/all_to_all | solution.py:252
  29.5 1.9 %pack_q.1 = bf16[8,128,256]{2,1,0:T(8,128)(2,1)} custom-call(bf16[128,2048]{1,0:T(8,128)(2,1)} %queries), custom_call_target="tpu_custom_call" | custom-call | flops 8589934592 | bytes 16777216 | tf_op jit(solution)/shard_map/pack_q/pallas_call | solution.py:87
  31.4 4.2 %all-to-all-start.1 = ((bf16[8,128,256]{2,1,0:T(8,128)(2,1)}), bf16[8,128,256]{2,1,0:T(8,128)(2,1)S(1)}, u32[]{:S(2)}, u32[]{:S(2)}) async-start(bf16[8,128,256]{2,1,0:T(8,128)(2,1)} %pack_q.1), calls=%async_computation.1 | async-start | bytes 1048576 | tf_op jit(solution)/shard_map/all_to_all | solution.py:252
  35.5 9.0 %collective-permute-start.1 = (bf16[8,272,256]{2,1,0:T(8,128)(2,1)S(1)}, bf16[8,272,256]{2,1,0:T(8,128)(2,1)S(1)}, u32[]{:S(2)}, u32[]{:S(2)}) collective-permute-start(bf16[8,272,256]{2,1,0:T(8,128)(2,1)S(1)} %all_to_all.15.kv), channel_id=1, source_target_pairs={{0,504},{8,0},{16,8},{24,16},{32,24},{40,32},{48,40},{56,48},{64,5... | collective-permute-start | bytes 3342344 | tf_op jit(solution)/shard_map/ppermute | solution.py:257
  44.6 1.9 %collective-permute-start = (bf16[8,272,256]{2,1,0:T(8,128)(2,1)S(1)}, bf16[8,272,256]{2,1,0:T(8,128)(2,1)}, u32[]{:S(2)}, u32[]{:S(2)}) collective-permute-start(bf16[8,272,256]{2,1,0:T(8,128)(2,1)S(1)} %all_to_all.15.kv), channel_id=1, source_target_pairs={{0,8},{8,16},{16,24},{24,32},{32,40},{40,48},{48,56},{56,64},{64,7... | collective-permute-start | bytes 3342344 | tf_op jit(solution)/shard_map/ppermute | solution.py:257
  46.5 0.1 pad_add_fusion.place
  46.6 0.0 all-to-all-done.1.qs
  46.6 3.6 %own_block.1 = (f32[1024,128]{1,0:T(8,128)S(1)}, f32[1024,256]{1,0:T(8,128)S(1)}, f32[1024,256]{1,0:T(8,128)S(1)}, f32[1024,256]{1,0:T(8,128)S(1)}) custom-call(bf16[8,272,256]{2,1,0:T(8,128)(2,1)S(1)} %all_to_all.15.kv, bf16[8,128,256]{2,1,0:T(8,128)(2,1)S(1)} %all-to-all-done.1.qs), custom_call_target="tpu_custom_call" | custom-call | flops 8589934592 | bytes 16777216 | tf_op jit(solution)/shard_map/own_block/pallas_call | solution.py:182
  50.2 18.2 %collective-permute-done.1.down = bf16[8,272,256]{2,1,0:T(8,128)(2,1)S(1)} collective-permute-done((bf16[8,272,256]{2,1,0:T(8,128)(2,1)S(1)}, bf16[8,272,256]{2,1,0:T(8,128)(2,1)S(1)}, u32[]{:S(2)}, u32[]{:S(2)}) %collective-permute-start.1) | collective-permute-done | bytes 1114144 | tf_op jit(solution)/shard_map/ppermute | solution.py:257
  68.4 7.2 %collective-permute-done.up = bf16[8,272,256]{2,1,0:T(8,128)(2,1)} collective-permute-done((bf16[8,272,256]{2,1,0:T(8,128)(2,1)S(1)}, bf16[8,272,256]{2,1,0:T(8,128)(2,1)}, u32[]{:S(2)}, u32[]{:S(2)}) %collective-permute-start) | collective-permute-done | bytes 1114144 | tf_op jit(solution)/shard_map/ppermute | solution.py:257
  75.6 3.9 %near_blocks.1 = bf16[8,128,256]{2,1,0:T(8,128)(2,1)S(1)} custom-call(s32[2]{0:T(128)S(1)} %pad_add_fusion.place, bf16[8,272,256]{2,1,0:T(8,128)(2,1)} %collective-permute-done.up, bf16[8,272,256]{2,1,0:T(8,128)(2,1)S(1)} %collective-permute-done.1.down, bf16[8,128,256]{2,1,0:T(8,128)(2,1)S(1)} %all-to-all-done.1.qs, ...), custom_call_target="tpu_custom_call" | custom-call | flops 3221225472 | bytes 6291456 | tf_op jit(solution)/shard_map/near_blocks/pallas_call | solution.py:239
  79.5 14.9 %all_to_all.16.parts = bf16[8,128,256]{2,1,0:T(8,128)(2,1)S(1)} all-to-all(bf16[8,128,256]{2,1,0:T(8,128)(2,1)S(1)} %near_blocks.1), channel_id=1, replica_groups=mesh['seq'=64,'head'=8] {'head'}, dimensions={0} | all-to-all | bytes 1048576 | tf_op jit(solution)/shard_map/all_to_all | solution.py:252
  94.4 0.8 unpack.1
Async XLA Ops:
  31.4 15.2 %all-to-all-start.1 = ((bf16[8,128,256]{2,1,0:T(8,128)(2,1)}), bf16[8,128,256]{2,1,0:T(8,128)(2,1)S(1)}, u32[]{:S(2)}, u32[]{:S(2)}) async-start(bf16[8,128,256]{2,1,0:T(8,128)(2,1)} %pack_q.1), calls=%async_computation.1 | async-start | bytes 1048576 | tf_op jit(solution)/shard_map/all_to_all | solution.py:252
  35.5 32.8 %collective-permute-start.1 = (bf16[8,272,256]{2,1,0:T(8,128)(2,1)S(1)}, bf16[8,272,256]{2,1,0:T(8,128)(2,1)S(1)}, u32[]{:S(2)}, u32[]{:S(2)}) collective-permute-start(bf16[8,272,256]{2,1,0:T(8,128)(2,1)S(1)} %all_to_all.15.kv), channel_id=1, source_target_pairs={{0,504},{8,0},{16,8},{24,16},{32,24},{40,32},{48,40},{56,48},{64,5... | collective-permute-start | bytes 3342344 | tf_op jit(solution)/shard_map/ppermute | solution.py:257
  44.6 31.0 %collective-permute-start = (bf16[8,272,256]{2,1,0:T(8,128)(2,1)S(1)}, bf16[8,272,256]{2,1,0:T(8,128)(2,1)}, u32[]{:S(2)}, u32[]{:S(2)}) collective-permute-start(bf16[8,272,256]{2,1,0:T(8,128)(2,1)S(1)} %all_to_all.15.kv), channel_id=1, source_target_pairs={{0,8},{8,16},{16,24},{24,32},{32,40},{40,48},{48,56},{56,64},{64,7... | collective-permute-start | bytes 3342344 | tf_op jit(solution)/shard_map/ppermute | solution.py:257

commit v2 on v1

--- a/solution.py
+++ b/solution.py
@@ -1,3 +1,4 @@
+import functools
 import math
 
 import jax
@@ -17,7 +18,9 @@
 BLOCK = PARTS * ROWS
 TILE = 2 * ROWS
 TILES = BLOCK // TILE
+SPAN = 2
 BIG = 1e30
+HEADROOM = 60.0
 EXP2_SCALE = math.log2(math.e) / math.sqrt(HD)
 HBM = pl.BlockSpec(memory_space=pltpu.HBM)
 ANY = pl.BlockSpec(memory_space=pl.ANY)
@@ -90,8 +93,8 @@
         in_specs=[HBM],
         out_specs=VMEM,
         scratch_shapes=[pltpu.SemaphoreType.DMA((PARTS,))],
-        compiler_params=pltpu.CompilerParams(vmem_limit_bytes=61 * 1024 * 1024),
-        cost_estimate=estimate(8),
+        compiler_params=LIMIT,
+        cost_estimate=estimate(0),
         name="pack_q",
     )(queries)
 
@@ -186,86 +189,157 @@
         out_specs=[VMEM] * 4,
         scratch_shapes=[pltpu.VMEM((HEADS, TILE, BLOCK), F32)],
         compiler_params=LIMIT,
-        cost_estimate=estimate(8),
+        cost_estimate=estimate(0),
         name="own_block",
     )(kv, qs)
 
 
-def near_kernel(place, up, down, qs, q_ids, own_sum, own_total, own_max, out, sum_, total, top_):
-    sum_[...] = jnp.zeros_like(sum_)
-    total[...] = jnp.zeros_like(total)
-    top_[...] = jnp.full_like(top_, -BIG)
+def span_rows(ref, k, part, h):
+    return jnp.concatenate([tile_rows(ref, k * SPAN + i, part, h) for i in range(SPAN)], axis=0)
+
+
+def spread(value, count):
+    return jnp.concatenate([value] * count, axis=1)
+
+
+def near_kernel(final, ref, qs, q_ids, sum_in, total_in, max_in, *rest):
+    if final:
+        ready, out, sums, totals, tops, excess = rest
+    else:
+        sums, totals, tops, out, excess = rest
+    spans = range(TILES // SPAN)
     lows = [jnp.max(q_ids[t * TILE : t * TILE + 1, :]) for t in range(TILES)]
     highs = [jnp.max(q_ids[(t + 1) * TILE - 1 : (t + 1) * TILE, :]) for t in range(TILES)]
-    ids = [[tile_ids(ref, k) for k in range(TILES)] for ref in (up, down)]
-    lasts = [jnp.max(row) for row in ids[0]]
-    firsts = [jnp.min(row) for row in ids[1]]
-    for side, ref in enumerate((up, down)):
-        for k in range(TILES):
-            k_ids = ids[side][k]
-            for t in range(TILES):
-                rows = slice(t * TILE, (t + 1) * TILE)
-                if side:
-                    live = (firsts[k] <= highs[t]) & (place[0] < place[1] - 1)
-                else:
-                    live = (lasts[k] >= lows[t]) & (place[0] > 0)
-
-                @pl.when(live)
-                def _(ref=ref, k=k, t=t, rows=rows, k_ids=k_ids):
-                    bias = jnp.where(wide(q_ids[rows, :]) == k_ids, 0.0, -BIG)
+    ids = [
+        jnp.concatenate([tile_ids(ref, k * SPAN + i) for i in range(SPAN)], axis=1) for k in spans
+    ]
+    firsts = [jnp.min(row) for row in ids]
+    lasts = [jnp.max(row) for row in ids]
+    excess[...] = jnp.full_like(excess, -BIG)
+    lives = [
+        [(firsts[k] <= highs[t]) & (lasts[k] >= lows[t]) for k in spans] for t in range(TILES)
+    ]
+    active = [functools.reduce(jnp.logical_or, lives[t]) for t in range(TILES)]
+
+    def masked_scores(t, k, h, bias):
+        return scores_of(query_rows(qs, t, h), span_rows(ref, k, 0, h)) + bias
+
+    def bias_of(rows, k):
+        return jnp.where(spread(q_ids[rows, :], 2 * SPAN) == ids[k], 0.0, -BIG)
+
+    def best_of(part):
+        return functools.reduce(
+            jnp.maximum, [part[:, c * HD : (c + 1) * HD] for c in range(2 * SPAN)]
+        )
+
+    def copy_state(rows):
+        sums[rows, :] = sum_in[rows, :]
+        totals[rows, :] = total_in[rows, :]
+        tops[rows, :] = max_in[rows, :]
+
+    def finish(t, rows):
+        result = (sums[rows, :] / totals[rows, :]).astype(BF16)
+        for i in range(2):
+            out[2 * t + i] = result[i * ROWS : (i + 1) * ROWS, :]
+
+    for t in range(TILES):
+        rows = slice(t * TILE, (t + 1) * TILE)
+        if not final:
+            copy_state(rows)
+
+        @pl.when(active[t])
+        def _(t=t, rows=rows):
+            if final:
+                copy_state(rows)
+            for k in spans:
+
+                @pl.when(lives[t][k])
+                def _(k=k):
+                    bias = bias_of(rows, k)
                     for h in range(HEADS):
                         cols = head_cols(h)
-                        scores = scores_of(query_rows(qs, t, h), tile_rows(ref, k, 0, h)) + bias
-                        old = top_[rows, cols]
-                        new = jnp.maximum(old, jnp.max(scores, axis=1, keepdims=True))
-                        factor = jnp.exp2((old - new) * EXP2_SCALE)
-                        weights = jnp.exp2((scores - wide(new)) * EXP2_SCALE)
-                        both = weigh(weights, tile_rows(ref, k, 1, h))
-                        sum_[rows, cols] = sum_[rows, cols] * factor + both[:, :HD]
-                        total[rows, cols] = total[rows, cols] * factor + both[:, HD:]
-                        top_[rows, cols] = new
-
-    for p in range(PARTS):
-        rows = slice(p * ROWS, (p + 1) * ROWS)
-        best = jnp.maximum(top_[rows, :], own_max[rows, :])
-        far = jnp.exp2((top_[rows, :] - best) * EXP2_SCALE)
-        near = jnp.exp2((own_max[rows, :] - best) * EXP2_SCALE)
-        value = near * own_sum[rows, :] + far * sum_[rows, :]
-        scale = near * own_total[rows, :] + far * total[rows, :]
-        out[p] = (value / scale).astype(BF16)
-
-
-def near_blocks(place, up, down, qs, state):
-    return pl.pallas_call(
-        near_kernel,
-        out_shape=jax.ShapeDtypeStruct((PARTS, ROWS, WIDE), BF16),
-        in_specs=[SMEM] + [VMEM] * 7,
-        out_specs=VMEM,
-        scratch_shapes=[pltpu.VMEM((BLOCK, WIDE), F32)] * 3,
+                        above = masked_scores(t, k, h, bias) - spread(max_in[rows, cols], 2 * SPAN)
+                        excess[...] = jnp.maximum(excess[...], best_of(above))
+                        both = weigh(jnp.exp2(above * EXP2_SCALE), span_rows(ref, k, 1, h))
+                        sums[rows, cols] += both[:, :HD]
+                        totals[rows, cols] += both[:, HD:]
+
+    @pl.when(jnp.max(excess[...]) * EXP2_SCALE > HEADROOM)
+    def _():
+        for t in range(TILES):
+            rows = slice(t * TILE, (t + 1) * TILE)
+
+            @pl.when(active[t])
+            def _(t=t, rows=rows):
+                copy_state(rows)
+                for k in spans:
+
+                    @pl.when(lives[t][k])
+                    def _(k=k):
+                        bias = bias_of(rows, k)
+                        for h in range(HEADS):
+                            cols = head_cols(h)
+                            part = masked_scores(t, k, h, bias)
+                            old = tops[rows, cols]
+                            new = jnp.max(best_of(part), axis=1, keepdims=True)
+                            new = jnp.maximum(old, new)
+                            factor = jnp.exp2((old - new) * EXP2_SCALE)
+                            part = jnp.exp2((part - spread(new, 2 * SPAN)) * EXP2_SCALE)
+                            both = weigh(part, span_rows(ref, k, 1, h))
+                            sums[rows, cols] = sums[rows, cols] * factor + both[:, :HD]
+                            totals[rows, cols] = totals[rows, cols] * factor + both[:, HD:]
+                            tops[rows, cols] = new
+
+    for t in range(TILES):
+        rows = slice(t * TILE, (t + 1) * TILE)
+        if final:
+            pl.when(active[t])(functools.partial(finish, t, rows))
+
+            @pl.when(jnp.logical_not(active[t]))
+            def _(t=t):
+                for i in range(2):
+                    out[2 * t + i] = ready[2 * t + i]
+
+        else:
+            finish(t, rows)
+
+
+def near_block(final, ref, qs, q_ids, state, *ready):
+    state_shape = [jax.ShapeDtypeStruct((BLOCK, WIDE), F32)] * 3
+    result = jax.ShapeDtypeStruct((PARTS, ROWS, WIDE), BF16)
+    excess = pltpu.VMEM((TILE, HD), F32)
+    work = [pltpu.VMEM((BLOCK, WIDE), F32)] * 3
+    return pl.pallas_call(
+        functools.partial(near_kernel, final),
+        out_shape=result if final else state_shape + [result],
+        in_specs=[VMEM] * (6 + len(ready)),
+        out_specs=VMEM if final else [VMEM] * 4,
+        scratch_shapes=work + [excess] if final else [excess],
         compiler_params=LIMIT,
-        cost_estimate=estimate(3),
-        name="near_blocks",
-    )(place, up, down, qs, *state)
+        name="last_block" if final else "near_block",
+    )(ref, qs, q_ids, *state, *ready)
 
 
 def across_heads(value):
     return lax.all_to_all(value, "head", 0, 0, tiled=True)
 
 
-def across_blocks(value, step):
+def swapped(value, first):
     size = lax.axis_size("seq")
-    return lax.ppermute(value, "seq", [(i, (i + step) % size) for i in range(size)])
+    pairs = []
+    for i in range(first, size + first, 2):
+        pairs += [(i % size, (i + 1) % size), ((i + 1) % size, i % size)]
+    return lax.ppermute(value, "seq", pairs)
 
 
 def per_device(queries, keys, values, doc_ids):
-    count = jnp.int32(lax.axis_size("seq"))
-    place = jnp.stack([lax.axis_index("seq"), count]).astype(jnp.int32)
     kv = across_heads(pack_kv(doc_ids.reshape(1, ROWS), keys, values))
     kv, queries = lax.optimization_barrier((kv, queries))
-    up, down = across_blocks(kv, 1), across_blocks(kv, -1)
+    even, odd = swapped(kv, 0), swapped(kv, 1)
     qs = across_heads(pack_q(queries))
-    state = own_block(kv, qs)
-    out = near_blocks(place, up, down, qs, state)
+    q_ids, *state = own_block(kv, qs)
+    *state, ready = near_block(False, odd, qs, q_ids, state)
+    out = near_block(True, even, qs, q_ids, state, ready)
     return unpack(across_heads(out))
 
 

time: 95.9 us -> 81.6 us (0.85)
  waiting for transfers between devices: 25.4 us -> 7.34 us
  blocking collectives: 41.3 us -> 53.3 us
  starting transfers between devices: 15.1 us -> 10.9 us
  Pallas kernels: 13.4 us -> 9.39 us
    ppermute x2, waiting for transfers between devices: 25.4 us -> 7.34 us  [swapped(): return lax.ppermute(value, 'seq', pairs)]
    all_to_all x2 -> x3, blocking collectives: 41.3 us -> 53.3 us  [across_heads(): return lax.all_to_all(value, 'head', 0, 0, tiled=True)]
    all_to_all x1 -> x0, starting transfers between devices: 4.15 us -> none  [across_heads(): return lax.all_to_all(value, 'head', 0, 0, tiled=True)]
    pallas_call x1 -> x2, Pallas kernels: 3.94 us -> 1.72 us  [near_block(): pl.pallas_call(functools.partial(near_kernel, final), out_shape=result if...]
    pallas_call x1, Pallas kernels: 1.93 us -> 0.17 us  [pack_q(): pl.pallas_call(pack_q_kernel, out_shape=jax.ShapeDtypeStruct((PARTS, ROWS...]
  transfers between devices with their start and end apart: 3 -> 2, of which waited for: 2 -> 2; matrix products, arithmetic and copies ran while one was open for 0% -> 0% of each run, Pallas kernels for 4% -> 6%
where the time goes in v2:
time: 81.6 us; the launch traced here: 81.2 us
  blocking collectives  53.3 us (65%)
  starting transfers between devices  10.9 us (13%)
  Pallas kernels  9.39 us (12%)
  waiting for transfers between devices  7.34 us (9%)
    all_to_all x3, blocking collectives, across_heads(): return lax.all_to_all(value, 'head', 0, 0, tiled=True)  53.3 us
    ppermute x2, starting transfers between devices, swapped(): return lax.ppermute(value, 'seq', pairs)  10.9 us
    ppermute x2, waiting for transfers between devices, swapped(): return lax.ppermute(value, 'seq', pairs)  7.34 us
    pallas_call x1, Pallas kernels, own_block(): pl.pallas_call(own_kernel, out_shape=[jax.ShapeDtypeStruct((BLOCK, ROWS),...  3.62 us
    pallas_call x1, Pallas kernels, pack_kv(): pl.pallas_call(pack_kv_kernel, out_shape=jax.ShapeDtypeStruct((PARTS, PIE...  3.03 us
    pallas_call x2, Pallas kernels, near_block(): pl.pallas_call(functools.partial(near_kernel, final), out_shape=result if...  1.72 us
  transfers between devices with their start and end apart: 2, of which 2 were waited for; matrix products, arithmetic and copies ran while one was open for 0% of the time, Pallas kernels for 6%

profile of v2, /device:TPU:1, one launch (start us, length us, event | category | flops | bytes accessed | tf_op | source)
XLA Modules:
  0.0 81.2 jit_solution(6798541376096055037)
XLA Ops:
  0.0 3.0 %pack_kv.1 = bf16[8,272,256]{2,1,0:T(8,128)(2,1)} custom-call(s32[1,128]{1,0:T(1,128)} %bitcast.1, bf16[128,2048]{1,0:T(8,128)(2,1)} %keys.1, bf16[128,2048]{1,0:T(8,128)(2,1)} %values.1), custom_call_target="tpu_custom_call" | custom-call | tf_op jit(solution)/shard_map/pack_kv/pallas_call | solution.py:70
  3.0 0.0 copy-start
  3.1 26.5 %all_to_all.15.kv = bf16[8,272,256]{2,1,0:T(8,128)(2,1)S(1)} all-to-all(bf16[8,272,256]{2,1,0:T(8,128)(2,1)} %pack_kv.1), channel_id=1, replica_groups=mesh['seq'=64,'head'=8] {'head'}, dimensions={0} | all-to-all | bytes 2228224 | tf_op jit(solution)/shard_map/all_to_all | solution.py:324
  29.6 9.0 %collective-permute-start.1 = (bf16[8,272,256]{2,1,0:T(8,128)(2,1)S(1)}, bf16[8,272,256]{2,1,0:T(8,128)(2,1)S(1)}, u32[]{:S(2)}, u32[]{:S(2)}) collective-permute-start(bf16[8,272,256]{2,1,0:T(8,128)(2,1)S(1)} %all_to_all.15.kv), channel_id=1, source_target_pairs={{8,16},{16,8},{24,32},{32,24},{40,48},{48,40},{56,64},{64,56},{72,... | collective-permute-start | bytes 3342344 | tf_op jit(solution)/shard_map/ppermute | solution.py:332
  38.6 1.9 %collective-permute-start = (bf16[8,272,256]{2,1,0:T(8,128)(2,1)S(1)}, bf16[8,272,256]{2,1,0:T(8,128)(2,1)S(1)}, u32[]{:S(2)}, u32[]{:S(2)}) collective-permute-start(bf16[8,272,256]{2,1,0:T(8,128)(2,1)S(1)} %all_to_all.15.kv), channel_id=1, source_target_pairs={{0,8},{8,0},{16,24},{24,16},{32,40},{40,32},{48,56},{56,48},{64,72... | collective-permute-start | bytes 3342344 | tf_op jit(solution)/shard_map/ppermute | solution.py:332
  40.6 0.0 copy-done
  40.6 0.2 pack_q.1
  40.7 13.1 %all_to_all.16.qs = bf16[8,128,256]{2,1,0:T(8,128)(2,1)S(1)} all-to-all(bf16[8,128,256]{2,1,0:T(8,128)(2,1)S(1)} %pack_q.1), channel_id=1, replica_groups=mesh['seq'=64,'head'=8] {'head'}, dimensions={0} | all-to-all | bytes 1048576 | tf_op jit(solution)/shard_map/all_to_all | solution.py:324
  53.8 3.6 %own_block.1 = (f32[1024,128]{1,0:T(8,128)S(1)}, f32[1024,256]{1,0:T(8,128)S(1)}, f32[1024,256]{1,0:T(8,128)S(1)}, f32[1024,256]{1,0:T(8,128)S(1)}) custom-call(bf16[8,272,256]{2,1,0:T(8,128)(2,1)S(1)} %all_to_all.15.kv, bf16[8,128,256]{2,1,0:T(8,128)(2,1)S(1)} %all_to_all.16.qs), custom_call_target="tpu_custom_call" | custom-call | tf_op jit(solution)/shard_map/own_block/pallas_call | solution.py:185
  57.4 5.4 %collective-permute-done.1.ref = bf16[8,272,256]{2,1,0:T(8,128)(2,1)S(1)} collective-permute-done((bf16[8,272,256]{2,1,0:T(8,128)(2,1)S(1)}, bf16[8,272,256]{2,1,0:T(8,128)(2,1)S(1)}, u32[]{:S(2)}, u32[]{:S(2)}) %collective-permute-start.1) | collective-permute-done | bytes 1114144 | tf_op jit(solution)/shard_map/ppermute | solution.py:332
  62.8 0.8 near_block.1
  63.6 2.0 %collective-permute-done.ref = bf16[8,272,256]{2,1,0:T(8,128)(2,1)S(1)} collective-permute-done((bf16[8,272,256]{2,1,0:T(8,128)(2,1)S(1)}, bf16[8,272,256]{2,1,0:T(8,128)(2,1)S(1)}, u32[]{:S(2)}, u32[]{:S(2)}) %collective-permute-start) | collective-permute-done | bytes 1114144 | tf_op jit(solution)/shard_map/ppermute | solution.py:332
  65.6 1.0 %last_block.1 = bf16[8,128,256]{2,1,0:T(8,128)(2,1)S(1)} custom-call(bf16[8,272,256]{2,1,0:T(8,128)(2,1)S(1)} %collective-permute-done.ref, bf16[8,128,256]{2,1,0:T(8,128)(2,1)S(1)} %all_to_all.16.qs, f32[1024,128]{1,0:T(8,128)S(1)} %get-tuple-element.17.q_ids, f32[1024,256]{1,0:T(8,128)S(1)} %get-tuple-element.21.sum_in, ...), custom_call_target="tpu_custom_call" | custom-call | tf_op jit(solution)/shard_map/last_block/pallas_call | solution.py:312
  66.5 13.7 %all_to_all.17.parts = bf16[8,128,256]{2,1,0:T(8,128)(2,1)S(1)} all-to-all(bf16[8,128,256]{2,1,0:T(8,128)(2,1)S(1)} %last_block.1), channel_id=1, replica_groups=mesh['seq'=64,'head'=8] {'head'}, dimensions={0} | all-to-all | bytes 1048576 | tf_op jit(solution)/shard_map/all_to_all | solution.py:324
  80.2 0.8 %unpack.1 = bf16[128,2048]{1,0:T(8,128)(2,1)} custom-call(bf16[8,128,256]{2,1,0:T(8,128)(2,1)S(1)} %all_to_all.17.parts), custom_call_target="tpu_custom_call" | custom-call | tf_op jit(solution)/shard_map/unpack/pallas_call | solution.py:109
Async XLA Ops:
  3.0 37.5 %copy-start = (bf16[128,2048]{1,0:T(8,128)(2,1)S(1)}, bf16[128,2048]{1,0:T(8,128)(2,1)}, u32[]{:S(2)}) copy-start(bf16[128,2048]{1,0:T(8,128)(2,1)} %queries) | copy-start | bytes 1572868
  29.6 33.2 %collective-permute-start.1 = (bf16[8,272,256]{2,1,0:T(8,128)(2,1)S(1)}, bf16[8,272,256]{2,1,0:T(8,128)(2,1)S(1)}, u32[]{:S(2)}, u32[]{:S(2)}) collective-permute-start(bf16[8,272,256]{2,1,0:T(8,128)(2,1)S(1)} %all_to_all.15.kv), channel_id=1, source_target_pairs={{8,16},{16,8},{24,32},{32,24},{40,48},{48,40},{56,64},{64,56},{72,... | collective-permute-start | bytes 3342344 | tf_op jit(solution)/shard_map/ppermute | solution.py:332
  38.6 26.9 %collective-permute-start = (bf16[8,272,256]{2,1,0:T(8,128)(2,1)S(1)}, bf16[8,272,256]{2,1,0:T(8,128)(2,1)S(1)}, u32[]{:S(2)}, u32[]{:S(2)}) collective-permute-start(bf16[8,272,256]{2,1,0:T(8,128)(2,1)S(1)} %all_to_all.15.kv), channel_id=1, source_target_pairs={{0,8},{8,0},{16,24},{24,16},{32,40},{40,32},{48,56},{56,48},{64,72... | collective-permute-start | bytes 3342344 | tf_op jit(solution)/shard_map/ppermute | solution.py:332

commit v3 on v2

--- a/solution.py
+++ b/solution.py
@@ -50,32 +50,43 @@
     return slice(p * WIDE, (p + 1) * WIDE)
 
 
-def pack_kv_kernel(ids, keys, values, kv, sems):
-    pairs = []
-    for p in range(PARTS):
-        pairs += [
-            (keys.at[:, part_cols(p)], kv.at[p, 0:ROWS]),
-            (values.at[:, part_cols(p)], kv.at[p, ROWS : 2 * ROWS]),
-        ]
-    copies = run_copies(pairs, sems)
+def pack_kv_kernel(ids, keys, values, kv):
     row = jnp.broadcast_to(ids[...].astype(F32), (TAGS, ROWS))
     tags = jnp.concatenate([row] * HEADS, axis=1).astype(BF16)
     for p in range(PARTS):
+        kv[p, 0:ROWS, :] = keys[:, part_cols(p)]
+        kv[p, ROWS : 2 * ROWS, :] = values[:, part_cols(p)]
         kv[p, 2 * ROWS : PIECE, :] = tags
-    for copy in copies:
-        copy.wait()
 
 
 def pack_kv(ids, keys, values):
     return pl.pallas_call(
         pack_kv_kernel,
         out_shape=jax.ShapeDtypeStruct((PARTS, PIECE, WIDE), BF16),
-        in_specs=[VMEM, HBM, HBM],
+        in_specs=[VMEM] * 3,
         out_specs=VMEM,
-        scratch_shapes=[pltpu.SemaphoreType.DMA((2 * PARTS,))],
-        compiler_params=pltpu.CompilerParams(vmem_limit_bytes=61 * 1024 * 1024),
+        compiler_params=LIMIT,
         name="pack_kv",
     )(ids, keys, values)
+
+
+def gather_kernel(parts, kv):
+    for p in range(PARTS):
+        kv[p * ROWS : (p + 1) * ROWS, :] = parts[p, 0:ROWS, :]
+        kv[BLOCK + p * ROWS : BLOCK + (p + 1) * ROWS, :] = parts[p, ROWS : 2 * ROWS, :]
+    rows = [parts[p, 2 * ROWS : PIECE, :].astype(F32)[0:1, :] for p in range(PARTS)]
+    kv[2 * BLOCK : 2 * BLOCK + TAGS, :] = jnp.concatenate(rows * 2, axis=0).astype(BF16)
+
+
+def gather(parts):
+    return pl.pallas_call(
+        gather_kernel,
+        out_shape=jax.ShapeDtypeStruct((2 * BLOCK + TAGS, WIDE), BF16),
+        in_specs=[VMEM],
+        out_specs=VMEM,
+        compiler_params=LIMIT,
+        name="gather",
+    )(parts)
 
 
 def pack_q_kernel(queries, qs, sems):
@@ -118,7 +129,7 @@
 
 
 def id_row(ref, p):
-    return ref[p, 2 * ROWS : PIECE, 0:ROWS].astype(F32)[0:1, :]
+    return ref[2 * BLOCK : 2 * BLOCK + TAGS, 0:ROWS].astype(F32)[p : p + 1, :]
 
 
 def down_rows(row):
@@ -129,9 +140,9 @@
     return jnp.concatenate([id_row(ref, 2 * tile), id_row(ref, 2 * tile + 1)], axis=1)
 
 
-def tile_rows(ref, tile, part, h):
-    rows = slice(part * ROWS, (part + 1) * ROWS)
-    return jnp.concatenate([ref[2 * tile + i, rows, head_cols(h)] for i in range(2)], axis=0)
+def tile_rows(ref, tile, part, h, count=1):
+    base = part * BLOCK + tile * TILE
+    return ref[base : base + count * TILE, head_cols(h)]
 
 
 def query_rows(ref, tile, h):
@@ -195,7 +206,7 @@
 
 
 def span_rows(ref, k, part, h):
-    return jnp.concatenate([tile_rows(ref, k * SPAN + i, part, h) for i in range(SPAN)], axis=0)
+    return tile_rows(ref, k * SPAN, part, h, SPAN)
 
 
 def spread(value, count):
@@ -333,13 +344,13 @@
 
 
 def per_device(queries, keys, values, doc_ids):
-    kv = across_heads(pack_kv(doc_ids.reshape(1, ROWS), keys, values))
+    kv = gather(across_heads(pack_kv(doc_ids.reshape(1, ROWS), keys, values)))
     kv, queries = lax.optimization_barrier((kv, queries))
     even, odd = swapped(kv, 0), swapped(kv, 1)
     qs = across_heads(pack_q(queries))
     q_ids, *state = own_block(kv, qs)
-    *state, ready = near_block(False, odd, qs, q_ids, state)
-    out = near_block(True, even, qs, q_ids, state, ready)
+    *state, ready = near_block(False, even, qs, q_ids, state)
+    out = near_block(True, odd, qs, q_ids, state, ready)
     return unpack(across_heads(out))
 
 

time: 81.6 us -> 78.7 us (0.964)
  waiting for transfers between devices: 7.34 us -> 2.31 us
  local copies, waits for them, and re-layouts: 0.01 us -> 2.74 us
  starting transfers between devices: 10.9 us -> 12.7 us
  blocking collectives: 53.3 us -> 52.1 us
  Pallas kernels: 9.39 us -> 8.26 us
    ppermute x2, waiting for transfers between devices: 7.34 us -> 2.31 us  [swapped(): return lax.ppermute(value, 'seq', pairs)]
    pallas_call x1, Pallas kernels: 3.03 us -> 0.08 us  [pack_kv(): pl.pallas_call(pack_kv_kernel, out_shape=jax.ShapeDtypeStruct((PARTS, PIE...]
    unnamed x2 -> x8, local copies, waits for them, and re-layouts: 0.01 us -> 2.74 us
    ppermute x2, starting transfers between devices: 10.9 us -> 12.7 us  [swapped(): return lax.ppermute(value, 'seq', pairs)]
    pallas_call x2, Pallas kernels: 1.72 us -> 3.34 us  [near_block(): pl.pallas_call(functools.partial(near_kernel, final), out_shape=result if...]
    all_to_all x3, blocking collectives: 53.3 us -> 52.1 us  [across_heads(): return lax.all_to_all(value, 'head', 0, 0, tiled=True)]
  transfers between devices with their start and end apart: 2 -> 2, of which waited for: 2 -> 1; matrix products, arithmetic and copies ran while one was open for 0% -> 0% of each run, Pallas kernels for 6% -> 9%
where the time goes in v3:
time: 78.7 us; the launch traced here: 78.3 us
  blocking collectives  52.1 us (66%)
  starting transfers between devices  12.7 us (16%)
  Pallas kernels  8.26 us (10%)
  local copies, waits for them, and re-layouts  2.74 us (3%)
  waiting for transfers between devices  2.31 us (3%)
    all_to_all x3, blocking collectives, across_heads(): return lax.all_to_all(value, 'head', 0, 0, tiled=True)  52.1 us
    ppermute x2, starting transfers between devices, swapped(): return lax.ppermute(value, 'seq', pairs)  12.7 us
    pallas_call x1, Pallas kernels, own_block(): pl.pallas_call(own_kernel, out_shape=[jax.ShapeDtypeStruct((BLOCK, ROWS),...  3.76 us
    pallas_call x2, Pallas kernels, near_block(): pl.pallas_call(functools.partial(near_kernel, final), out_shape=result if...  3.34 us
    unnamed x8, local copies, waits for them, and re-layouts  2.74 us
    ppermute x2, waiting for transfers between devices, swapped(): return lax.ppermute(value, 'seq', pairs)  2.31 us
  transfers between devices with their start and end apart: 2, of which 1 were waited for; matrix products, arithmetic and copies ran while one was open for 0% of the time, Pallas kernels for 9%

profile of v3, /device:TPU:1, one launch (start us, length us, event | category | flops | bytes accessed | tf_op | source)
XLA Modules:
  0.0 78.3 jit_solution(9348523009930760945)
XLA Ops:
  0.0 0.0 copy-start
  0.0 1.0 %copy-done = bf16[128,2048]{1,0:T(8,128)(2,1)S(1)} copy-done((bf16[128,2048]{1,0:T(8,128)(2,1)S(1)}, bf16[128,2048]{1,0:T(8,128)(2,1)}, u32[]{:S(2)}) %copy-start) | copy-done | bytes 524312
  1.0 0.0 copy-start.1
  1.0 1.0 %copy-done.1 = bf16[128,2048]{1,0:T(8,128)(2,1)S(1)} copy-done((bf16[128,2048]{1,0:T(8,128)(2,1)S(1)}, bf16[128,2048]{1,0:T(8,128)(2,1)}, u32[]{:S(2)}) %copy-start.1) | copy-done | bytes 524312
  2.1 0.0 copy-start.3
  2.1 0.7 copy-done.3
  2.7 0.1 pack_kv.1
  2.8 25.3 %all_to_all.15.parts = bf16[8,272,256]{2,1,0:T(8,128)(2,1)S(1)} all-to-all(bf16[8,272,256]{2,1,0:T(8,128)(2,1)S(1)} %pack_kv.1), channel_id=1, replica_groups=mesh['seq'=64,'head'=8] {'head'}, dimensions={0} | all-to-all | bytes 2228224 | tf_op jit(solution)/shard_map/all_to_all | solution.py:335
  28.2 0.0 copy-start.2
  28.2 0.1 gather.1.kv
  28.2 2.1 %collective-permute-start.1 = (bf16[2064,256]{1,0:T(8,128)(2,1)S(1)}, bf16[2064,256]{1,0:T(8,128)(2,1)S(1)}, u32[]{:S(2)}, u32[]{:S(2)}) collective-permute-start(bf16[2064,256]{1,0:T(8,128)(2,1)S(1)} %gather.1.kv), channel_id=1, source_target_pairs={{0,8},{8,0},{16,24},{24,16},{32,40},{40,32},{48,56},{56,48},{64,72... | collective-permute-start | bytes 3170312 | tf_op jit(solution)/shard_map/ppermute | solution.py:343
  30.3 10.6 %collective-permute-start = (bf16[2064,256]{1,0:T(8,128)(2,1)S(1)}, bf16[2064,256]{1,0:T(8,128)(2,1)S(1)}, u32[]{:S(2)}, u32[]{:S(2)}) collective-permute-start(bf16[2064,256]{1,0:T(8,128)(2,1)S(1)} %gather.1.kv), channel_id=1, source_target_pairs={{8,16},{16,8},{24,32},{32,24},{40,48},{48,40},{56,64},{64,56},{72,... | collective-permute-start | bytes 3170312 | tf_op jit(solution)/shard_map/ppermute | solution.py:343
  40.9 0.0 copy-done.2
  40.9 0.2 pack_q.1
  41.1 13.4 %all_to_all.16.qs = bf16[8,128,256]{2,1,0:T(8,128)(2,1)S(1)} all-to-all(bf16[8,128,256]{2,1,0:T(8,128)(2,1)S(1)} %pack_q.1), channel_id=1, replica_groups=mesh['seq'=64,'head'=8] {'head'}, dimensions={0} | all-to-all | bytes 1048576 | tf_op jit(solution)/shard_map/all_to_all | solution.py:335
  54.5 3.8 %own_block.1 = (f32[1024,128]{1,0:T(8,128)S(1)}, f32[1024,256]{1,0:T(8,128)S(1)}, f32[1024,256]{1,0:T(8,128)S(1)}, f32[1024,256]{1,0:T(8,128)S(1)}) custom-call(bf16[2064,256]{1,0:T(8,128)(2,1)S(1)} %gather.1.kv, bf16[8,128,256]{2,1,0:T(8,128)(2,1)S(1)} %all_to_all.16.qs), custom_call_target="tpu_custom_call" | custom-call | tf_op jit(solution)/shard_map/own_block/pallas_call | solution.py:196
  58.2 0.0 collective-permute-done.1.ref
  58.2 3.0 %near_block.1 = (f32[1024,256]{1,0:T(8,128)S(1)}, f32[1024,256]{1,0:T(8,128)S(1)}, f32[1024,256]{1,0:T(8,128)S(1)}, bf16[8,128,256]{2,1,0:T(8,128)(2,1)S(1)}) custom-call(bf16[2064,256]{1,0:T(8,128)(2,1)S(1)} %collective-permute-done.1.ref, bf16[8,128,256]{2,1,0:T(8,128)(2,1)S(1)} %all_to_all.16.qs, f32[1024,128]{1,0:T(8,128)S(1)} %get-tuple-element.17.q_ids, ...), custom_call_target="tpu_custom_call" | custom-call | tf_op jit(solution)/shard_map/near_block/pallas_call | solution.py:323
  61.3 2.3 %collective-permute-done.ref = bf16[2064,256]{1,0:T(8,128)(2,1)S(1)} collective-permute-done((bf16[2064,256]{1,0:T(8,128)(2,1)S(1)}, bf16[2064,256]{1,0:T(8,128)(2,1)S(1)}, u32[]{:S(2)}, u32[]{:S(2)}) %collective-permute-start) | collective-permute-done | bytes 1056800 | tf_op jit(solution)/shard_map/ppermute | solution.py:343
  63.6 0.3 last_block.1
  63.9 13.4 %all_to_all.17.parts = bf16[8,128,256]{2,1,0:T(8,128)(2,1)S(1)} all-to-all(bf16[8,128,256]{2,1,0:T(8,128)(2,1)S(1)} %last_block.1), channel_id=1, replica_groups=mesh['seq'=64,'head'=8] {'head'}, dimensions={0} | all-to-all | bytes 1048576 | tf_op jit(solution)/shard_map/all_to_all | solution.py:335
  77.3 0.8 %unpack.1 = bf16[128,2048]{1,0:T(8,128)(2,1)} custom-call(bf16[8,128,256]{2,1,0:T(8,128)(2,1)S(1)} %all_to_all.17.parts), custom_call_target="tpu_custom_call" | custom-call | tf_op jit(solution)/shard_map/unpack/pallas_call | solution.py:120
Async XLA Ops:
  0.0 1.0 %copy-start = (bf16[128,2048]{1,0:T(8,128)(2,1)S(1)}, bf16[128,2048]{1,0:T(8,128)(2,1)}, u32[]{:S(2)}) copy-start(bf16[128,2048]{1,0:T(8,128)(2,1)} %keys.1) | copy-start | bytes 1572868
  1.0 1.0 %copy-start.1 = (bf16[128,2048]{1,0:T(8,128)(2,1)S(1)}, bf16[128,2048]{1,0:T(8,128)(2,1)}, u32[]{:S(2)}) copy-start(bf16[128,2048]{1,0:T(8,128)(2,1)} %values.1) | copy-start | bytes 1572868
  2.1 0.7 copy-start.3
  28.2 12.8 %copy-start.2 = (bf16[128,2048]{1,0:T(8,128)(2,1)S(1)}, bf16[128,2048]{1,0:T(8,128)(2,1)}, u32[]{:S(2)}) copy-start(bf16[128,2048]{1,0:T(8,128)(2,1)} %queries) | copy-start | bytes 1572868
  28.2 30.0 %collective-permute-start.1 = (bf16[2064,256]{1,0:T(8,128)(2,1)S(1)}, bf16[2064,256]{1,0:T(8,128)(2,1)S(1)}, u32[]{:S(2)}, u32[]{:S(2)}) collective-permute-start(bf16[2064,256]{1,0:T(8,128)(2,1)S(1)} %gather.1.kv), channel_id=1, source_target_pairs={{0,8},{8,0},{16,24},{24,16},{32,40},{40,32},{48,56},{56,48},{64,72... | collective-permute-start | bytes 3170312 | tf_op jit(solution)/shard_map/ppermute | solution.py:343
  30.3 33.3 %collective-permute-start = (bf16[2064,256]{1,0:T(8,128)(2,1)S(1)}, bf16[2064,256]{1,0:T(8,128)(2,1)S(1)}, u32[]{:S(2)}, u32[]{:S(2)}) collective-permute-start(bf16[2064,256]{1,0:T(8,128)(2,1)S(1)} %gather.1.kv), channel_id=1, source_target_pairs={{8,16},{16,8},{24,32},{32,24},{40,48},{48,40},{56,64},{64,56},{72,... | collective-permute-start | bytes 3170312 | tf_op jit(solution)/shard_map/ppermute | solution.py:343

commit v4 on v3

--- a/solution.py
+++ b/solution.py
@@ -50,16 +50,34 @@
     return slice(p * WIDE, (p + 1) * WIDE)
 
 
-def pack_kv_kernel(ids, keys, values, kv):
-    row = jnp.broadcast_to(ids[...].astype(F32), (TAGS, ROWS))
-    tags = jnp.concatenate([row] * HEADS, axis=1).astype(BF16)
+def tag_kernel(ids, tags):
+    lane = lax.broadcasted_iota(jnp.int32, (TAGS, ROWS), 1)
+    row = jnp.zeros((TAGS, ROWS), jnp.int32)
+    for i in range(ROWS):
+        row = jnp.where(lane == i, ids[i], row)
+    tags[...] = jnp.concatenate([row.astype(F32)] * HEADS, axis=1).astype(BF16)
+
+
+def tag_rows(ids):
+    return pl.pallas_call(
+        tag_kernel,
+        out_shape=jax.ShapeDtypeStruct((TAGS, WIDE), BF16),
+        in_specs=[SMEM],
+        out_specs=VMEM,
+        compiler_params=LIMIT,
+        cost_estimate=estimate(4),
+        name="tag_rows",
+    )(ids)
+
+
+def pack_kv_kernel(tags, keys, values, kv):
     for p in range(PARTS):
         kv[p, 0:ROWS, :] = keys[:, part_cols(p)]
         kv[p, ROWS : 2 * ROWS, :] = values[:, part_cols(p)]
-        kv[p, 2 * ROWS : PIECE, :] = tags
-
-
-def pack_kv(ids, keys, values):
+        kv[p, 2 * ROWS : PIECE, :] = tags[...]
+
+
+def pack_kv(tags, keys, values):
     return pl.pallas_call(
         pack_kv_kernel,
         out_shape=jax.ShapeDtypeStruct((PARTS, PIECE, WIDE), BF16),
@@ -67,7 +85,7 @@
         out_specs=VMEM,
         compiler_params=LIMIT,
         name="pack_kv",
-    )(ids, keys, values)
+    )(tags, keys, values)
 
 
 def gather_kernel(parts, kv):
@@ -344,7 +362,7 @@
 
 
 def per_device(queries, keys, values, doc_ids):
-    kv = gather(across_heads(pack_kv(doc_ids.reshape(1, ROWS), keys, values)))
+    kv = gather(across_heads(pack_kv(tag_rows(doc_ids), keys, values)))
     kv, queries = lax.optimization_barrier((kv, queries))
     even, odd = swapped(kv, 0), swapped(kv, 1)
     qs = across_heads(pack_q(queries))

time: 78.7 us -> 77.2 us (0.981)
  local copies, waits for them, and re-layouts: 2.74 us -> 0.75 us
  waiting for transfers between devices: 2.31 us -> 3.44 us
    unnamed x8, local copies, waits for them, and re-layouts: 2.74 us -> 0.75 us
    ppermute x2, waiting for transfers between devices: 2.31 us -> 3.44 us  [swapped(): return lax.ppermute(value, 'seq', pairs)]
    pallas_call x2, Pallas kernels: 3.34 us -> 2.22 us  [near_block(): pl.pallas_call(functools.partial(near_kernel, final), out_shape=result if...]
  transfers between devices with their start and end apart: 2 -> 2, of which waited for: 1 -> 1; matrix products, arithmetic and copies ran while one was open for 0% -> 0% of each run, Pallas kernels for 9% -> 8%
where the time goes in v4:
time: 77.2 us; the launch traced here: 77 us
  blocking collectives  52.1 us (67%)
  starting transfers between devices  12.7 us (16%)
  Pallas kernels  7.76 us (10%)
  waiting for transfers between devices  3.44 us (4%)
    all_to_all x3, blocking collectives, across_heads(): return lax.all_to_all(value, 'head', 0, 0, tiled=True)  52.1 us
    ppermute x2, starting transfers between devices, swapped(): return lax.ppermute(value, 'seq', pairs)  12.7 us
    pallas_call x1, Pallas kernels, own_block(): pl.pallas_call(own_kernel, out_shape=[jax.ShapeDtypeStruct((BLOCK, ROWS),...  3.76 us
    ppermute x2, waiting for transfers between devices, swapped(): return lax.ppermute(value, 'seq', pairs)  3.44 us
    pallas_call x2, Pallas kernels, near_block(): pl.pallas_call(functools.partial(near_kernel, final), out_shape=result if...  2.22 us
  transfers between devices with their start and end apart: 2, of which 1 were waited for; matrix products, arithmetic and copies ran while one was open for 0% of the time, Pallas kernels for 8%

profile of v4, /device:TPU:1, one launch (start us, length us, event | category | flops | bytes accessed | tf_op | source)
XLA Modules:
  0.0 77.0 jit_solution(5734794704456740950)
XLA Ops:
  0.0 0.0 copy-start.2
  0.0 0.0 copy-start.1
  0.0 0.0 copy-start.3
  0.0 0.7 copy-done.3
  0.7 0.6 tag_rows.1.tags
  1.4 0.0 copy-done.2
  1.4 0.0 copy-done.1
  1.4 0.1 pack_kv.1
  1.5 25.3 %all_to_all.15.parts = bf16[8,272,256]{2,1,0:T(8,128)(2,1)S(1)} all-to-all(bf16[8,272,256]{2,1,0:T(8,128)(2,1)S(1)} %pack_kv.1), channel_id=1, replica_groups=mesh['seq'=64,'head'=8] {'head'}, dimensions={0} | all-to-all | bytes 2228224 | tf_op jit(solution)/shard_map/all_to_all | solution.py:353
  26.8 0.0 copy-start
  26.8 0.1 gather.1.kv
  26.9 2.1 %collective-permute-start.1 = (bf16[2064,256]{1,0:T(8,128)(2,1)S(1)}, bf16[2064,256]{1,0:T(8,128)(2,1)S(1)}, u32[]{:S(2)}, u32[]{:S(2)}) collective-permute-start(bf16[2064,256]{1,0:T(8,128)(2,1)S(1)} %gather.1.kv), channel_id=1, source_target_pairs={{0,8},{8,0},{16,24},{24,16},{32,40},{40,32},{48,56},{56,48},{64,72... | collective-permute-start | bytes 3170312 | tf_op jit(solution)/shard_map/ppermute | solution.py:361
  28.9 10.6 %collective-permute-start = (bf16[2064,256]{1,0:T(8,128)(2,1)S(1)}, bf16[2064,256]{1,0:T(8,128)(2,1)S(1)}, u32[]{:S(2)}, u32[]{:S(2)}) collective-permute-start(bf16[2064,256]{1,0:T(8,128)(2,1)S(1)} %gather.1.kv), channel_id=1, source_target_pairs={{8,16},{16,8},{24,32},{32,24},{40,48},{48,40},{56,64},{64,56},{72,... | collective-permute-start | bytes 3170312 | tf_op jit(solution)/shard_map/ppermute | solution.py:361
  39.6 0.0 copy-done
  39.6 0.2 pack_q.1
  39.8 13.4 %all_to_all.16.qs = bf16[8,128,256]{2,1,0:T(8,128)(2,1)S(1)} all-to-all(bf16[8,128,256]{2,1,0:T(8,128)(2,1)S(1)} %pack_q.1), channel_id=1, replica_groups=mesh['seq'=64,'head'=8] {'head'}, dimensions={0} | all-to-all | bytes 1048576 | tf_op jit(solution)/shard_map/all_to_all | solution.py:353
  53.1 3.8 %own_block.1 = (f32[1024,128]{1,0:T(8,128)S(1)}, f32[1024,256]{1,0:T(8,128)S(1)}, f32[1024,256]{1,0:T(8,128)S(1)}, f32[1024,256]{1,0:T(8,128)S(1)}) custom-call(bf16[2064,256]{1,0:T(8,128)(2,1)S(1)} %gather.1.kv, bf16[8,128,256]{2,1,0:T(8,128)(2,1)S(1)} %all_to_all.16.qs), custom_call_target="tpu_custom_call" | custom-call | tf_op jit(solution)/shard_map/own_block/pallas_call | solution.py:214
  56.9 0.0 collective-permute-done.1.ref
  56.9 1.9 %near_block.1 = (f32[1024,256]{1,0:T(8,128)S(1)}, f32[1024,256]{1,0:T(8,128)S(1)}, f32[1024,256]{1,0:T(8,128)S(1)}, bf16[8,128,256]{2,1,0:T(8,128)(2,1)S(1)}) custom-call(bf16[2064,256]{1,0:T(8,128)(2,1)S(1)} %collective-permute-done.1.ref, bf16[8,128,256]{2,1,0:T(8,128)(2,1)S(1)} %all_to_all.16.qs, f32[1024,128]{1,0:T(8,128)S(1)} %get-tuple-element.17.q_ids, ...), custom_call_target="tpu_custom_call" | custom-call | tf_op jit(solution)/shard_map/near_block/pallas_call | solution.py:341
  58.8 3.4 %collective-permute-done.ref = bf16[2064,256]{1,0:T(8,128)(2,1)S(1)} collective-permute-done((bf16[2064,256]{1,0:T(8,128)(2,1)S(1)}, bf16[2064,256]{1,0:T(8,128)(2,1)S(1)}, u32[]{:S(2)}, u32[]{:S(2)}) %collective-permute-start) | collective-permute-done | bytes 1056800 | tf_op jit(solution)/shard_map/ppermute | solution.py:361
  62.2 0.3 last_block.1
  62.6 13.4 %all_to_all.17.parts = bf16[8,128,256]{2,1,0:T(8,128)(2,1)S(1)} all-to-all(bf16[8,128,256]{2,1,0:T(8,128)(2,1)S(1)} %last_block.1), channel_id=1, replica_groups=mesh['seq'=64,'head'=8] {'head'}, dimensions={0} | all-to-all | bytes 1048576 | tf_op jit(solution)/shard_map/all_to_all | solution.py:353
  76.0 0.8 %unpack.1 = bf16[128,2048]{1,0:T(8,128)(2,1)} custom-call(bf16[8,128,256]{2,1,0:T(8,128)(2,1)S(1)} %all_to_all.17.parts), custom_call_target="tpu_custom_call" | custom-call | tf_op jit(solution)/shard_map/unpack/pallas_call | solution.py:138
Async XLA Ops:
  0.0 1.4 %copy-start.2 = (bf16[128,2048]{1,0:T(8,128)(2,1)S(1)}, bf16[128,2048]{1,0:T(8,128)(2,1)}, u32[]{:S(2)}) copy-start(bf16[128,2048]{1,0:T(8,128)(2,1)} %values.1) | copy-start | bytes 1572868
  0.0 1.4 %copy-start.1 = (bf16[128,2048]{1,0:T(8,128)(2,1)S(1)}, bf16[128,2048]{1,0:T(8,128)(2,1)}, u32[]{:S(2)}) copy-start(bf16[128,2048]{1,0:T(8,128)(2,1)} %keys.1) | copy-start | bytes 1572868
  0.0 0.7 copy-start.3
  26.8 12.8 %copy-start = (bf16[128,2048]{1,0:T(8,128)(2,1)S(1)}, bf16[128,2048]{1,0:T(8,128)(2,1)}, u32[]{:S(2)}) copy-start(bf16[128,2048]{1,0:T(8,128)(2,1)} %queries) | copy-start | bytes 1572868
  26.9 30.0 %collective-permute-start.1 = (bf16[2064,256]{1,0:T(8,128)(2,1)S(1)}, bf16[2064,256]{1,0:T(8,128)(2,1)S(1)}, u32[]{:S(2)}, u32[]{:S(2)}) collective-permute-start(bf16[2064,256]{1,0:T(8,128)(2,1)S(1)} %gather.1.kv), channel_id=1, source_target_pairs={{0,8},{8,0},{16,24},{24,16},{32,40},{40,32},{48,56},{56,48},{64,72... | collective-permute-start | bytes 3170312 | tf_op jit(solution)/shard_map/ppermute | solution.py:361
  28.9 33.3 %collective-permute-start = (bf16[2064,256]{1,0:T(8,128)(2,1)S(1)}, bf16[2064,256]{1,0:T(8,128)(2,1)S(1)}, u32[]{:S(2)}, u32[]{:S(2)}) collective-permute-start(bf16[2064,256]{1,0:T(8,128)(2,1)S(1)} %gather.1.kv), channel_id=1, source_target_pairs={{8,16},{16,8},{24,32},{32,24},{40,48},{48,40},{56,64},{64,56},{72,... | collective-permute-start | bytes 3170312 | tf_op jit(solution)/shard_map/ppermute | solution.py:361
